TPU v7x, 256 devices: a whole 4x4x8 slice. The times are simulated.
256 devices in a mesh: ea: 128 (over y, z, x), ta: 2 (over core).
Axes of the slice: x: 4, y: 4, z: 8, core: 2. Of those that a mesh axis runs over, the one named last changes fastest.
Arguments:
- sample_inphase: float32 [128, 256, 256], P('ea'), may hold values from 0.2 to 1.2
- sample_quadrature: float32 [128, 256, 256], P('ea'), may hold values from -3 to 3
- beam_inphase: float32 [128, 3, 32, 32], P('ea'), may hold values from -3 to 3
- beam_quadrature: float32 [128, 3, 32, 32], P('ea'), may hold values from -3 to 3
- recorded_diffraction: float32 [128, 2, 16, 32, 32], P('ea', 'ta'), may hold values from 0.05 to 4
- window_corners: int32 [128, 2, 16, 2], P('ea', 'ta'), may hold values from 0 to 224
- filled_tallies: int32 [128, 2], P('ea', 'ta'), may hold values from 1 to 16, 24 in all within a row
- absorption_templates: float32 [16, 128], replicated, may hold values from -6 to 6
Outputs:
- fitted: float32 [2, 128, 128, 2, 256], P(None, 'ea', None, 'ta')
- coefficients: float32 [2, 16, 65536], P(None, None, ('ea', 'ta'))
Inputs may be any that keep to these rules, and one draw needn't show every extreme that they name: `filled_tallies`: in each energy the two tiles' counts sum to 24 and the larger is at most 16. `window_corners`: offsets of slots at or past their tile's count are not used.
All inputs are finite; a program needn't handle non-finite values. No bound on the sum of `filled_tallies` on one device may be relied on, other than what follows from the above.
Results may differ from a plain program's by a relative error of at most 0.0003.
Values sent between devices are 32-bit elements; how exact they have to be, the bound alone decides.
A program may use at most 64 MiB of HBM per device.

v0:
```python
import jax
import jax.numpy as jnp
from jax import lax
from jax.sharding import PartitionSpec as P

HIGHEST_PRECISION = lax.Precision.HIGHEST
FLOOR_POWER = 0.5
REGULARIZER = 1.0


def dft_tables(length):
    counter = jnp.arange(length, dtype=jnp.int32)
    product = counter[:, None] * counter[None, :] % length
    angles = 2.0 * jnp.pi / length * product.astype(jnp.float32)
    norming = 1.0 / jnp.sqrt(jnp.float32(length))
    return (jnp.cos(angles) * norming, -jnp.sin(angles) * norming)


def two_sided(field_re, field_im, table_re, table_im):
    left_re = jnp.einsum(
        "jk,...kl->...jl", table_re, field_re, precision=HIGHEST_PRECISION
    ) - jnp.einsum("jk,...kl->...jl", table_im, field_im, precision=HIGHEST_PRECISION)
    left_im = jnp.einsum(
        "jk,...kl->...jl", table_re, field_im, precision=HIGHEST_PRECISION
    ) + jnp.einsum("jk,...kl->...jl", table_im, field_re, precision=HIGHEST_PRECISION)
    right_re = jnp.einsum(
        "...jk,kl->...jl", left_re, table_re, precision=HIGHEST_PRECISION
    ) - jnp.einsum("...jk,kl->...jl", left_im, table_im, precision=HIGHEST_PRECISION)
    right_im = jnp.einsum(
        "...jk,kl->...jl", left_re, table_im, precision=HIGHEST_PRECISION
    ) + jnp.einsum("...jk,kl->...jl", left_im, table_re, precision=HIGHEST_PRECISION)
    return (right_re, right_im)


def slot_terms(
    sample_inphase,
    sample_quadrature,
    beam_inphase,
    beam_quadrature,
    intensity,
    corners,
    weight,
    table_re,
    table_im,
):
    width = beam_inphase.shape[-1]

    def extract(source, corner):
        return lax.dynamic_slice(source, (corner[0], corner[1]), (width, width))

    patch_re = jax.vmap(extract, (None, 0))(sample_inphase, corners)
    patch_im = jax.vmap(extract, (None, 0))(sample_quadrature, corners)
    exit_re = beam_inphase[None] * patch_re[:, None] - beam_quadrature[None] * patch_im[:, None]
    exit_im = beam_inphase[None] * patch_im[:, None] + beam_quadrature[None] * patch_re[:, None]
    far_re, far_im = two_sided(exit_re, exit_im, table_re, table_im)
    power = jnp.sum(far_re * far_re + far_im * far_im, axis=1)
    factor = (1.0 - jnp.sqrt(intensity) / jnp.sqrt(jnp.maximum(power, FLOOR_POWER))) * weight[
        :, None, None
    ]
    back_re, back_im = two_sided(
        far_re * factor[:, None], far_im * factor[:, None], table_re, -table_im
    )
    terms_re = jnp.sum(beam_inphase[None] * back_re + beam_quadrature[None] * back_im, axis=1)
    terms_im = jnp.sum(beam_inphase[None] * back_im - beam_quadrature[None] * back_re, axis=1)
    return (terms_re, terms_im)


def deposit(field, patch, corner):
    width = patch.shape[0]
    current = lax.dynamic_slice(field, (corner[0], corner[1]), (width, width))
    return lax.dynamic_update_slice(field, current + patch, (corner[0], corner[1]))


def local(
    sample_inphase,
    sample_quadrature,
    beam_inphase,
    beam_quadrature,
    recorded_diffraction,
    window_corners,
    filled_tallies,
    absorption_templates,
):
    local_energies = sample_inphase.shape[0]
    side = sample_inphase.shape[1]
    spot_numbering = recorded_diffraction.shape[2]
    width = beam_inphase.shape[-1]
    blocks = lax.axis_size("ea")
    tiles = lax.axis_size("ta")
    tile = lax.axis_index("ta")
    table_re, table_im = dft_tables(width)
    group = 8
    first_slot = jnp.zeros((local_energies,), jnp.int32)
    taken_slots = filled_tallies[:, 0]
    tile_boundary = jnp.full((local_energies,), spot_numbering, jnp.int32)
    gathered_recordings = recorded_diffraction[:, 0]
    pooled_offsets = window_corners[:, 0]

    def lone_wavelength(items):
        o_re, o_im, p_re, p_im, intensity_pool, corner_pool, start, number, split = items
        light_patch = jnp.sum(p_re * p_re + p_im * p_im, axis=0)
        zeros = jnp.zeros((side, side), jnp.float32)

        def advance(index, carry):
            grad_re, grad_im, light = carry
            position = start + index * group + jnp.arange(group, dtype=jnp.int32)
            weight = (position < start + number).astype(jnp.float32)
            source = jnp.where(position < split, position, spot_numbering + position - split)
            source = jnp.clip(source, 0, intensity_pool.shape[0] - 1)
            corners = corner_pool[source]
            terms_re, terms_im = slot_terms(
                o_re, o_im, p_re, p_im, intensity_pool[source], corners, weight, table_re, table_im
            )
            for member in range(group):
                grad_re = deposit(grad_re, terms_re[member], corners[member])
                grad_im = deposit(grad_im, terms_im[member], corners[member])
                light = deposit(light, light_patch * weight[member], corners[member])
            return (grad_re, grad_im, light)

        rounds = (number + group - 1) // group
        return lax.fori_loop(0, rounds, advance, (zeros, zeros, zeros))

    grad_re, grad_im, light = lax.map(
        lone_wavelength,
        (
            sample_inphase,
            sample_quadrature,
            beam_inphase,
            beam_quadrature,
            gathered_recordings,
            pooled_offsets,
            first_slot,
            taken_slots,
            tile_boundary,
        ),
    )

    def shares(field):
        return field.reshape(local_energies, blocks, tiles, -1)

    summed = lax.psum_scatter(
        jnp.stack([shares(grad_re), shares(grad_im), shares(light)]),
        "ta",
        scatter_dimension=3,
        tiled=True,
    )
    light_share = summed[2]
    own_re = lax.dynamic_slice_in_dim(shares(sample_inphase), tile, 1, 2)
    own_im = lax.dynamic_slice_in_dim(shares(sample_quadrature), tile, 1, 2)
    revised_inphase = own_re - summed[0] / (light_share + REGULARIZER)
    revised_quadrature = own_im - summed[1] / (light_share + REGULARIZER)
    spectra = jnp.stack([revised_inphase, revised_quadrature])[:, :, :, 0, :]
    gram = jnp.dot(absorption_templates, absorption_templates.T, precision=HIGHEST_PRECISION)
    factor_low = jnp.linalg.cholesky(gram)
    project = jax.scipy.linalg.cho_solve((factor_low, True), absorption_templates)
    values = lax.all_to_all(spectra, "ea", split_axis=2, concat_axis=1, tiled=True)[:, :, 0, :]
    coefs = jnp.einsum("ke,cen->ckn", project, values, precision=HIGHEST_PRECISION)
    fitted_here = jnp.einsum(
        "ke,ckn->cen", absorption_templates, coefs, precision=HIGHEST_PRECISION
    )
    returned = lax.all_to_all(
        fitted_here[:, :, None, :], "ea", split_axis=1, concat_axis=2, tiled=True
    )
    coef_local = coefs[:, :, None, :]
    return (returned[:, :, :, None, :], coef_local[:, :, 0, :])


def solution(mesh):
    in_specs = (
        P("ea", None, None),
        P("ea", None, None),
        P("ea", None, None, None),
        P("ea", None, None, None),
        P("ea", "ta", None, None, None),
        P("ea", "ta", None, None),
        P("ea", "ta"),
        P(),
    )
    out_specs = (P(None, "ea", None, "ta", None), P(None, None, ("ea", "ta")))
    return jax.shard_map(local, mesh=mesh, in_specs=in_specs, out_specs=out_specs, check_vma=False)
```

profile of v0, /device:TPU:2, one launch (start us, length us, event | category | flops | bytes accessed | tf_op | source)
XLA Modules:
  0.0 321.7 jit_solution(4731289166006635438)
XLA Ops:
  10.6 216.4 %while.42 = (s32[]{:T(128)}, f32[256,256]{1,0:T(8,128)S(1)}, f32[256,256]{1,0:T(8,128)S(1)}, f32[256,256]{1,0:T(8,128)S(1)}, s32[]{:T(128)}, /*index=5*/s32[16,2...) while((s32[]{:T(128)}, f32[256,256]{1,0:T(8,128)S(1)}, ...), condition=%wide.region_5.6_spmd.clone.clone, body=%wide.region_1.5_spmd.clone.clone.sunk | while | flops 152179840 | bytes 5044471 | solution.py:121
  18.2 1.1 dynamic_update_slice.335
  29.1 1.1 dynamic_update_slice.337
  34.5 1.1 dynamic_update_slice.338
  57.4 14.9 %while.44 = (s32[]{:T(128)}, f32[256,256]{1,0:T(8,128)S(1)}, s32[8,2]{0,1:T(2,128)S(1)}, f32[8,32,32]{2,1,0:T(8,128)S(1)}, s32[]{:T(128)}) while((s32[]{:T(128)}, f32[256,256]{1,0:T(8,128)S(1)}, s32[8,2]{0,1:T(2,128)S(1)}, f32[8,32,32]{2,1,0:T(8,128)S(1)}, s32[]{:T(128)}) %tuple.143), condition=%wide.while_cond, body=%wide.while_body.sunk | while | flops 2 | bytes 32877 | solution.py:49
  58.0 1.3 bitcast_dynamic-update-slice_fusion.5
  59.9 1.3 bitcast_dynamic-update-slice_fusion.5
  61.7 1.3 bitcast_dynamic-update-slice_fusion.5
  63.6 1.3 bitcast_dynamic-update-slice_fusion.5
  65.5 1.3 bitcast_dynamic-update-slice_fusion.5
  67.3 1.3 bitcast_dynamic-update-slice_fusion.5
  69.2 1.3 bitcast_dynamic-update-slice_fusion.5
  71.0 1.3 bitcast_dynamic-update-slice_fusion.5
  72.3 14.9 %while.43 = (s32[]{:T(128)}, f32[256,256]{1,0:T(8,128)S(1)}, s32[8,2]{0,1:T(2,128)S(1)}, f32[8,32,32]{2,1,0:T(8,128)S(1)}, s32[]{:T(128)}) while((s32[]{:T(128)}, f32[256,256]{1,0:T(8,128)S(1)}, s32[8,2]{0,1:T(2,128)S(1)}, f32[8,32,32]{2,1,0:T(8,128)S(1)}, s32[]{:T(128)}) %tuple.153), condition=%wide.while_cond.1, body=%wide.while_body.1.sunk | while | flops 2 | bytes 32877 | solution.py:49
  72.9 1.3 bitcast_dynamic-update-slice_fusion.4
  74.8 1.3 bitcast_dynamic-update-slice_fusion.4
  76.7 1.3 bitcast_dynamic-update-slice_fusion.4
  78.5 1.3 bitcast_dynamic-update-slice_fusion.4
  80.4 1.3 bitcast_dynamic-update-slice_fusion.4
  82.2 1.3 bitcast_dynamic-update-slice_fusion.4
  84.1 1.3 bitcast_dynamic-update-slice_fusion.4
  86.0 1.3 bitcast_dynamic-update-slice_fusion.4
  100.9 1.1 dynamic_update_slice.327
  107.6 1.1 dynamic_update_slice.333
  109.6 1.1 dynamic_update_slice.319
  112.0 1.1 dynamic_update_slice.321
  113.2 1.1 dynamic_update_slice.322
  116.3 1.1 dynamic_update_slice.325
  131.3 1.1 dynamic_update_slice.336
  142.3 1.1 dynamic_update_slice.338
  147.8 1.1 dynamic_update_slice.339
  164.1 1.1 dynamic_update_slice.342
  165.4 14.9 %while.44 = (s32[]{:T(128)}, f32[256,256]{1,0:T(8,128)S(1)}, s32[8,2]{0,1:T(2,128)S(1)}, f32[8,32,32]{2,1,0:T(8,128)S(1)}, s32[]{:T(128)}) while((s32[]{:T(128)}, f32[256,256]{1,0:T(8,128)S(1)}, s32[8,2]{0,1:T(2,128)S(1)}, f32[8,32,32]{2,1,0:T(8,128)S(1)}, s32[]{:T(128)}) %tuple.143), condition=%wide.while_cond, body=%wide.while_body.sunk | while | flops 2 | bytes 32877 | solution.py:49
  166.0 1.3 bitcast_dynamic-update-slice_fusion.5
  167.9 1.3 bitcast_dynamic-update-slice_fusion.5
  169.7 1.3 bitcast_dynamic-update-slice_fusion.5
  171.6 1.3 bitcast_dynamic-update-slice_fusion.5
  173.5 1.3 bitcast_dynamic-update-slice_fusion.5
  175.3 1.3 bitcast_dynamic-update-slice_fusion.5
  177.2 1.3 bitcast_dynamic-update-slice_fusion.5
  179.0 1.3 bitcast_dynamic-update-slice_fusion.5
  180.3 14.9 %while.43 = (s32[]{:T(128)}, f32[256,256]{1,0:T(8,128)S(1)}, s32[8,2]{0,1:T(2,128)S(1)}, f32[8,32,32]{2,1,0:T(8,128)S(1)}, s32[]{:T(128)}) while((s32[]{:T(128)}, f32[256,256]{1,0:T(8,128)S(1)}, s32[8,2]{0,1:T(2,128)S(1)}, f32[8,32,32]{2,1,0:T(8,128)S(1)}, s32[]{:T(128)}) %tuple.153), condition=%wide.while_cond.1, body=%wide.while_body.1.sunk | while | flops 2 | bytes 32877 | solution.py:49
  180.9 1.3 bitcast_dynamic-update-slice_fusion.4
  182.8 1.3 bitcast_dynamic-update-slice_fusion.4
  184.7 1.3 bitcast_dynamic-update-slice_fusion.4
  186.5 1.3 bitcast_dynamic-update-slice_fusion.4
  188.4 1.3 bitcast_dynamic-update-slice_fusion.4
  190.2 1.3 bitcast_dynamic-update-slice_fusion.4
  192.1 1.3 bitcast_dynamic-update-slice_fusion.4
  194.0 1.3 bitcast_dynamic-update-slice_fusion.4
  208.9 1.1 dynamic_update_slice.327
  210.1 1.1 dynamic_update_slice.328
  211.3 1.1 dynamic_update_slice.329
  212.5 1.1 dynamic_update_slice.330
  213.7 1.1 dynamic_update_slice.331
  217.9 1.1 dynamic_update_slice.319
  219.1 1.1 dynamic_update_slice.320
  229.6 1.5 cholesky.16
  233.0 28.8 %all-reduce.3.cloned.1.call-done = f32[3,1,128,2,256]{4,2,3,1,0:T(8,128)} async-done(((f32[3,1,128,2,256]{4,2,3,1,0:T(8,128)}), f32[3,1,128,2,256]{4,2,3,1,0:T(8,128)}) %all-reduce.3.cloned.1.call-update) | async-done | bytes 786448
  261.8 1.7 constant_dynamic-slice_fusion.3
  264.9 13.8 %all-to-all-start = ((f32[2,1,128,256]{3,0,1,2:T(2,128)}), f32[2,1,128,256]{3,0,1,2:T(2,128)S(1)}, u32[]{:S(2)}, u32[]{:S(2)}) async-start(f32[2,1,128,256]{3,0,1,2:T(2,128)} %maximum_bitcast_fusion), calls=%async_computation | async-start | bytes 524288 | tf_op jit(solution)/shard_map/all_to_all | solution.py:156
  279.3 1.2 custom-call.10
  280.9 12.0 %all-to-all-done = f32[2,1,128,256]{3,0,1,2:T(2,128)S(1)} async-done(((f32[2,1,128,256]{3,0,1,2:T(2,128)}), f32[2,1,128,256]{3,0,1,2:T(2,128)S(1)}, u32[]{:S(2)}, u32[]{:S(2)}) %all-to-all-start) | async-done | bytes 262176 | tf_op jit(solution)/shard_map/all_to_all | solution.py:156
  294.0 19.9 %all_to_all.8 = f32[2,128,1,256]{3,0,2,1:T(2,128)S(1)} all-to-all(f32[2,128,1,256]{3,0,2,1:T(2,128)S(1)} %copy.85), channel_id=1, replica_groups=mesh['ea'=128,'ta'=2] {'ea'}, dimensions={1} | all-to-all | bytes 524288 | tf_op jit(solution)/shard_map/all_to_all | solution.py:161
  (245 shorter events, 104.9 us)
Async XLA Ops:
  7.2 222.2 %copy-start = (f32[16,128]{1,0:T(8,128)S(1)}, f32[16,128]{1,0:T(8,128)}, u32[]{:S(2)}) copy-start(f32[16,128]{1,0:T(8,128)} %param.17) | copy-start | bytes 24580
  7.2 254.6 %all-reduce.3.cloned.1.call-start = ((), (), s32[]{:S(2)}) async-start(), calls=%async_computation.2 | async-start | bytes 1572864
  7.9 0.7 copy-start.7
  8.7 1.0 copy-start.5
  9.5 1.0 copy-start.4
  9.6 1.0 copy-start.3
  9.6 1.0 copy-start.1
  9.6 1.0 copy-start.2
  231.1 0.7 copy-start.8
  264.9 28.0 %all-to-all-start = ((f32[2,1,128,256]{3,0,1,2:T(2,128)}), f32[2,1,128,256]{3,0,1,2:T(2,128)S(1)}, u32[]{:S(2)}, u32[]{:S(2)}) async-start(f32[2,1,128,256]{3,0,1,2:T(2,128)} %maximum_bitcast_fusion), calls=%async_computation | async-start | bytes 524288 | tf_op jit(solution)/shard_map/all_to_all | solution.py:156
  293.2 0.6 copy-start.6
Sparse Core Ops, SparseCore 0:
  229.0 32.7 all-reduce.2
where the time goes:
time: 325 us; the launch traced here: 322 us
  local copies, waits for them, and re-layouts  122 us (38%)
  loops' own time  60.9 us (19%)
  waiting for transfers between devices  40.8 us (13%)
  matrix products  27 us (8%)
  other arithmetic  22.7 us (7%)
  blocking collectives  19.9 us (6%)
  between operations  14.9 us (5%)
  starting transfers between devices  13.8 us (4%)
    another operation x1, loops' own time, lone_wavelength(): return lax.fori_loop(0, rounds, advance, (zeros, zeros, zeros))  60.8 us
    gather x96, local copies, waits for them, and re-layouts  59.5 us
    dynamic_update_slice x48, local copies, waits for them, and re-layouts, deposit(): lax.dynamic_update_slice(field, current + patch, (corner[0], corner[1]))  48.8 us
    unnamed x2, waiting for transfers between devices  28.8 us
    all_to_all x1, blocking collectives, local(): lax.all_to_all(fitted_here[:, :, None, :], 'ea', split_axis=1, concat_axi...  19.9 us
    add x46, other arithmetic, deposit(): current + patch  14.2 us
    all_to_all x1, starting transfers between devices, local(): lax.all_to_all(spectra, 'ea', split_axis=2, concat_axis=1, tiled=True)  13.8 us
    all_to_all x1, waiting for transfers between devices, local(): lax.all_to_all(spectra, 'ea', split_axis=2, concat_axis=1, tiled=True)  12 us
  transfers between devices with their start and end apart: 2, of which 2 were waited for; matrix products, arithmetic and copies ran while one was open for 2% of the time, Pallas kernels for 0%

commit v1 on v0

--- a/solution.py
+++ b/solution.py
@@ -158,8 +158,14 @@
     fitted_here = jnp.einsum(
         "ke,ckn->cen", absorption_templates, coefs, precision=HIGHEST_PRECISION
     )
-    returned = lax.all_to_all(
-        fitted_here[:, :, None, :], "ea", split_axis=1, concat_axis=2, tiled=True
+    returned = jnp.concatenate(
+        lax.all_to_all(
+            jnp.stack(jnp.split(fitted_here[:, :, None, :], lax.axis_size("ea"), axis=1)),
+            "ea",
+            0,
+            0,
+        ),
+        axis=2,
     )
     coef_local = coefs[:, :, None, :]
     return (returned[:, :, :, None, :], coef_local[:, :, 0, :])

time: 325 us -> 326 us (level)
  no operation moved by 1% of the time
where the time goes in v1:
time: 326 us; the launch traced here: 323 us
  local copies, waits for them, and re-layouts  123 us (38%)
  loops' own time  60.9 us (19%)
  waiting for transfers between devices  40.8 us (13%)
  matrix products  26.9 us (8%)
  other arithmetic  22.7 us (7%)
  blocking collectives  19.9 us (6%)
  between operations  15.3 us (5%)
  starting transfers between devices  13.8 us (4%)
    another operation x1, loops' own time, lone_wavelength(): return lax.fori_loop(0, rounds, advance, (zeros, zeros, zeros))  60.8 us
    gather x96, local copies, waits for them, and re-layouts  59.5 us
    dynamic_update_slice x48, local copies, waits for them, and re-layouts, deposit(): lax.dynamic_update_slice(field, current + patch, (corner[0], corner[1]))  48.8 us
    unnamed x2, waiting for transfers between devices  28.8 us
    all_to_all x1, blocking collectives, local(): lax.all_to_all(jnp.stack(jnp.split(fitted_here[:, :, None, :], lax.axis_s...  19.9 us
    add x46, other arithmetic, deposit(): current + patch  14.2 us
    all_to_all x1, starting transfers between devices, local(): lax.all_to_all(spectra, 'ea', split_axis=2, concat_axis=1, tiled=True)  13.8 us
    all_to_all x1, waiting for transfers between devices, local(): lax.all_to_all(spectra, 'ea', split_axis=2, concat_axis=1, tiled=True)  12 us
  transfers between devices with their start and end apart: 2, of which 2 were waited for; matrix products, arithmetic and copies ran while one was open for 2% of the time, Pallas kernels for 0%

profile of v1, /device:TPU:2, one launch (start us, length us, event | category | flops | bytes accessed | tf_op | source)
XLA Modules:
  0.0 323.3 jit_solution(16939474478106843490)
XLA Ops:
  10.6 216.4 %while.42 = (s32[]{:T(128)}, f32[256,256]{1,0:T(8,128)S(1)}, f32[256,256]{1,0:T(8,128)S(1)}, f32[256,256]{1,0:T(8,128)S(1)}, s32[]{:T(128)}, /*index=5*/s32[16,2...) while((s32[]{:T(128)}, f32[256,256]{1,0:T(8,128)S(1)}, ...), condition=%wide.region_5.6_spmd.clone.clone, body=%wide.region_1.5_spmd.clone.clone.sunk | while | flops 152179840 | bytes 5044471 | solution.py:121
  18.2 1.1 dynamic_update_slice.335
  29.1 1.1 dynamic_update_slice.337
  34.5 1.1 dynamic_update_slice.338
  57.4 14.9 %while.44 = (s32[]{:T(128)}, f32[256,256]{1,0:T(8,128)S(1)}, s32[8,2]{0,1:T(2,128)S(1)}, f32[8,32,32]{2,1,0:T(8,128)S(1)}, s32[]{:T(128)}) while((s32[]{:T(128)}, f32[256,256]{1,0:T(8,128)S(1)}, s32[8,2]{0,1:T(2,128)S(1)}, f32[8,32,32]{2,1,0:T(8,128)S(1)}, s32[]{:T(128)}) %tuple.143), condition=%wide.while_cond, body=%wide.while_body.sunk | while | flops 2 | bytes 32877 | solution.py:49
  58.0 1.3 bitcast_dynamic-update-slice_fusion.5
  59.9 1.3 bitcast_dynamic-update-slice_fusion.5
  61.7 1.3 bitcast_dynamic-update-slice_fusion.5
  63.6 1.3 bitcast_dynamic-update-slice_fusion.5
  65.5 1.3 bitcast_dynamic-update-slice_fusion.5
  67.3 1.3 bitcast_dynamic-update-slice_fusion.5
  69.2 1.3 bitcast_dynamic-update-slice_fusion.5
  71.0 1.3 bitcast_dynamic-update-slice_fusion.5
  72.3 14.9 %while.43 = (s32[]{:T(128)}, f32[256,256]{1,0:T(8,128)S(1)}, s32[8,2]{0,1:T(2,128)S(1)}, f32[8,32,32]{2,1,0:T(8,128)S(1)}, s32[]{:T(128)}) while((s32[]{:T(128)}, f32[256,256]{1,0:T(8,128)S(1)}, s32[8,2]{0,1:T(2,128)S(1)}, f32[8,32,32]{2,1,0:T(8,128)S(1)}, s32[]{:T(128)}) %tuple.153), condition=%wide.while_cond.1, body=%wide.while_body.1.sunk | while | flops 2 | bytes 32877 | solution.py:49
  72.9 1.3 bitcast_dynamic-update-slice_fusion.4
  74.8 1.3 bitcast_dynamic-update-slice_fusion.4
  76.7 1.3 bitcast_dynamic-update-slice_fusion.4
  78.5 1.3 bitcast_dynamic-update-slice_fusion.4
  80.4 1.3 bitcast_dynamic-update-slice_fusion.4
  82.2 1.3 bitcast_dynamic-update-slice_fusion.4
  84.1 1.3 bitcast_dynamic-update-slice_fusion.4
  86.0 1.3 bitcast_dynamic-update-slice_fusion.4
  100.9 1.1 dynamic_update_slice.327
  107.6 1.1 dynamic_update_slice.333
  109.6 1.1 dynamic_update_slice.319
  112.0 1.1 dynamic_update_slice.321
  113.2 1.1 dynamic_update_slice.322
  116.3 1.1 dynamic_update_slice.325
  131.3 1.1 dynamic_update_slice.336
  142.3 1.1 dynamic_update_slice.338
  147.8 1.1 dynamic_update_slice.339
  164.1 1.1 dynamic_update_slice.342
  165.4 14.9 %while.44 = (s32[]{:T(128)}, f32[256,256]{1,0:T(8,128)S(1)}, s32[8,2]{0,1:T(2,128)S(1)}, f32[8,32,32]{2,1,0:T(8,128)S(1)}, s32[]{:T(128)}) while((s32[]{:T(128)}, f32[256,256]{1,0:T(8,128)S(1)}, s32[8,2]{0,1:T(2,128)S(1)}, f32[8,32,32]{2,1,0:T(8,128)S(1)}, s32[]{:T(128)}) %tuple.143), condition=%wide.while_cond, body=%wide.while_body.sunk | while | flops 2 | bytes 32877 | solution.py:49
  166.0 1.3 bitcast_dynamic-update-slice_fusion.5
  167.9 1.3 bitcast_dynamic-update-slice_fusion.5
  169.7 1.3 bitcast_dynamic-update-slice_fusion.5
  171.6 1.3 bitcast_dynamic-update-slice_fusion.5
  173.5 1.3 bitcast_dynamic-update-slice_fusion.5
  175.3 1.3 bitcast_dynamic-update-slice_fusion.5
  177.2 1.3 bitcast_dynamic-update-slice_fusion.5
  179.0 1.3 bitcast_dynamic-update-slice_fusion.5
  180.3 14.9 %while.43 = (s32[]{:T(128)}, f32[256,256]{1,0:T(8,128)S(1)}, s32[8,2]{0,1:T(2,128)S(1)}, f32[8,32,32]{2,1,0:T(8,128)S(1)}, s32[]{:T(128)}) while((s32[]{:T(128)}, f32[256,256]{1,0:T(8,128)S(1)}, s32[8,2]{0,1:T(2,128)S(1)}, f32[8,32,32]{2,1,0:T(8,128)S(1)}, s32[]{:T(128)}) %tuple.153), condition=%wide.while_cond.1, body=%wide.while_body.1.sunk | while | flops 2 | bytes 32877 | solution.py:49
  180.9 1.3 bitcast_dynamic-update-slice_fusion.4
  182.8 1.3 bitcast_dynamic-update-slice_fusion.4
  184.7 1.3 bitcast_dynamic-update-slice_fusion.4
  186.5 1.3 bitcast_dynamic-update-slice_fusion.4
  188.4 1.3 bitcast_dynamic-update-slice_fusion.4
  190.2 1.3 bitcast_dynamic-update-slice_fusion.4
  192.1 1.3 bitcast_dynamic-update-slice_fusion.4
  194.0 1.3 bitcast_dynamic-update-slice_fusion.4
  208.9 1.1 dynamic_update_slice.327
  210.1 1.1 dynamic_update_slice.328
  211.3 1.1 dynamic_update_slice.329
  212.5 1.1 dynamic_update_slice.330
  213.7 1.1 dynamic_update_slice.331
  217.9 1.1 dynamic_update_slice.319
  219.1 1.1 dynamic_update_slice.320
  229.6 1.5 cholesky.16
  233.0 28.8 %all-reduce.3.cloned.1.call-done = f32[3,1,128,2,256]{4,2,3,1,0:T(8,128)} async-done(((f32[3,1,128,2,256]{4,2,3,1,0:T(8,128)}), f32[3,1,128,2,256]{4,2,3,1,0:T(8,128)}) %all-reduce.3.cloned.1.call-update) | async-done | bytes 786448
  261.8 1.7 constant_dynamic-slice_fusion.3
  264.9 13.8 %all-to-all-start = ((f32[2,1,128,256]{3,0,1,2:T(2,128)}), f32[2,1,128,256]{3,0,1,2:T(2,128)S(1)}, u32[]{:S(2)}, u32[]{:S(2)}) async-start(f32[2,1,128,256]{3,0,1,2:T(2,128)} %maximum_bitcast_fusion), calls=%async_computation | async-start | bytes 524288 | tf_op jit(solution)/shard_map/all_to_all | solution.py:156
  279.3 1.2 custom-call.10
  280.9 12.0 %all-to-all-done = f32[2,1,128,256]{3,0,1,2:T(2,128)S(1)} async-done(((f32[2,1,128,256]{3,0,1,2:T(2,128)}), f32[2,1,128,256]{3,0,1,2:T(2,128)S(1)}, u32[]{:S(2)}, u32[]{:S(2)}) %all-to-all-start) | async-done | bytes 262176 | tf_op jit(solution)/shard_map/all_to_all | solution.py:156
  295.6 19.9 %all_to_all.14 = f32[128,2,1,1,256]{4,2,3,1,0:T(1,128)S(1)} all-to-all(f32[128,2,1,1,256]{4,2,3,1,0:T(1,128)S(1)} %constant_dynamic-update-slice_fusion), channel_id=1, replica_groups=mesh['ea'=128,'ta'=2] {'ea'}, dimensions={0} | all-to-all | bytes 524288 | tf_op jit(solution)/shard_map/all_to_all | solution.py:162
  (372 shorter events, 106.2 us)
Async XLA Ops:
  7.2 222.2 %copy-start = (f32[16,128]{1,0:T(8,128)S(1)}, f32[16,128]{1,0:T(8,128)}, u32[]{:S(2)}) copy-start(f32[16,128]{1,0:T(8,128)} %param.17) | copy-start | bytes 24580
  7.2 254.6 %all-reduce.3.cloned.1.call-start = ((), (), s32[]{:S(2)}) async-start(), calls=%async_computation.2 | async-start | bytes 1572864
  7.9 0.7 copy-start.7
  8.7 1.0 copy-start.5
  9.5 1.0 copy-start.4
  9.6 1.0 copy-start.3
  9.6 1.0 copy-start.1
  9.6 1.0 copy-start.2
  231.1 0.7 copy-start.8
  264.9 28.0 %all-to-all-start = ((f32[2,1,128,256]{3,0,1,2:T(2,128)}), f32[2,1,128,256]{3,0,1,2:T(2,128)S(1)}, u32[]{:S(2)}, u32[]{:S(2)}) async-start(f32[2,1,128,256]{3,0,1,2:T(2,128)} %maximum_bitcast_fusion), calls=%async_computation | async-start | bytes 524288 | tf_op jit(solution)/shard_map/all_to_all | solution.py:156
  293.2 0.6 copy-start.6
Sparse Core Ops, SparseCore 0:
  229.0 32.7 all-reduce.2
